TPU v7x, 512 devices: a whole 4x8x8 slice. The times are simulated.
512 devices in a mesh: prow: 32 (over x, z), pcol: 16 (over y, core).
Axes of the slice: x: 4, y: 8, z: 8, core: 2. Of those that a mesh axis runs over, the one named last changes fastest.
Arguments:
- inverse_block: float32 [4, 32, 128, 8, 16, 128], P(None, 'prow', None, None, 'pcol'), may hold values from -6 to 6
- panel_first: float32 [4, 32, 256, 128], P(None, 'prow', 'pcol'), may hold values from -0.046875 to 0.046875
- panel_second: float32 [4, 32, 256, 128], P(None, 'prow', 'pcol'), may hold values from -0.046875 to 0.046875
- coupling: float32 [256, 256], P('prow'), may hold values from -0.375 to 0.375
- dinv_first: float32 [256, 256], replicated, may hold values from -6 to 6
- dinv_second: float32 [256, 256], replicated, may hold values from -6 to 6
- struct_first: int32 [128], replicated, may hold values 0 or 1
- struct_second: int32 [128], replicated, may hold values 0 or 1
Outputs:
- row_first: float32 [8, 16, 256, 128], P(None, 'pcol', 'prow')
- own_first: float32 [256, 256], replicated
- row_second: float32 [8, 16, 256, 128], P(None, 'pcol', 'prow')
- cross: float32 [256, 256], replicated
- own_second: float32 [256, 256], replicated
Inputs may be any that keep to these rules, and one draw needn't show every extreme that they name: `struct_first`: 1 marks a block that lies in the supernode's structure, 0 one that does not. `struct_second`: 1 marks a block that lies in the supernode's structure, 0 one that does not.
All inputs are finite; a program needn't handle non-finite values.
Results may differ from a plain program's by a relative error of at most 0.000084.
Values sent between devices are 32-bit elements; how exact they have to be, the bound alone decides.
A program may use at most 64 MiB of HBM per device.

v0:
```python
import jax
import jax.numpy as jnp
from jax import lax
from jax.sharding import PartitionSpec as P


def body(
    inverse_block,
    panel_first,
    panel_second,
    coupling,
    dinv_first,
    dinv_second,
    struct_first,
    struct_second,
):
    highest = lax.Precision.HIGHEST
    rows = lax.axis_size("prow")
    cols = lax.axis_size("pcol")
    prow_index = lax.axis_index("prow")
    pcol_index = lax.axis_index("pcol")
    ratio = rows // cols
    row_blocks = inverse_block.shape[0]
    blk = inverse_block.shape[2]
    col_blocks = inverse_block.shape[3]
    slab = coupling.shape[0]
    width = coupling.shape[1]
    local = inverse_block.reshape(row_blocks, blk, col_blocks, blk)
    diagonal = (prow_index % cols == pcol_index).astype(jnp.float32)

    def row_mask(struct):
        table = struct.astype(jnp.float32).reshape(row_blocks, rows)
        return lax.dynamic_slice_in_dim(table, prow_index, 1, 1)[:, :, None]

    def col_mask(struct):
        table = struct.astype(jnp.float32).reshape(col_blocks, cols)
        return lax.dynamic_slice_in_dim(table, pcol_index, 1, 1)[:, :, None]

    def matching(full):
        grouped = full.reshape(row_blocks, ratio, width, blk)
        return lax.dynamic_slice_in_dim(grouped, prow_index // cols, 1, 1)[:, 0]

    def my_rows(full):
        return lax.dynamic_slice_in_dim(full, prow_index * slab, slab, 1)

    def product(panel, mask):
        return jnp.einsum("rwx,rxcy->cwy", panel * mask, local, precision=highest)

    panel_a = lax.all_gather(panel_first, "pcol", axis=2, tiled=True)[:, 0]
    panel_b = lax.all_gather(panel_second, "pcol", axis=2, tiled=True)[:, 0]
    coupling_full = lax.all_gather(coupling, "prow", axis=0, tiled=True)
    rmask_a = row_mask(struct_first)
    rmask_b = row_mask(struct_second)
    cmask_a = col_mask(struct_first)
    cmask_b = col_mask(struct_second)
    part_a = product(panel_a, rmask_a)
    part_b = product(panel_b, rmask_b)
    row_a = -lax.psum(part_a, "prow") * cmask_a
    carried = jnp.einsum("av,cay->cvy", coupling, my_rows(row_a), precision=highest)
    row_b = -lax.psum(part_b + carried, "prow") * cmask_b
    chosen_a = matching(row_a)
    chosen_b = matching(row_b)
    mine_a = my_rows(row_a)
    mine_b = my_rows(row_b)
    term_a = jnp.einsum("rwy,rvy->wv", chosen_a, panel_a, precision=highest) * diagonal
    column_a = lax.psum(term_a, "prow")
    own_a = dinv_first - lax.psum(column_a, "pcol")
    own_rows = lax.dynamic_slice_in_dim(own_a, prow_index * slab, slab, 0)
    cross_term = (
        jnp.einsum("rvy,ray->va", panel_b * rmask_b, chosen_a, precision=highest)
        + jnp.einsum("av,aw->vw", coupling, own_rows, precision=highest)
    ) * diagonal
    own_term = jnp.einsum("rvy,ruy->vu", chosen_b, panel_b, precision=highest) * diagonal
    cross_col, own_col = lax.psum((cross_term, own_term), "prow")
    cross_sum, own_sum = lax.psum((cross_col, own_col), "pcol")
    cross = -cross_sum
    own_b = dinv_second - own_sum - jnp.dot(cross, coupling_full, precision=highest)
    out_a = mine_a.reshape(col_blocks, 1, slab, blk)
    out_b = mine_b.reshape(col_blocks, 1, slab, blk)
    return (out_a, own_a, out_b, cross, own_b)


def solution(mesh):
    return jax.shard_map(
        body,
        mesh=mesh,
        in_specs=(
            P(None, "prow", None, None, "pcol", None),
            P(None, "prow", "pcol", None),
            P(None, "prow", "pcol", None),
            P("prow", None),
            P(),
            P(),
            P(),
            P(),
        ),
        out_specs=(P(None, "pcol", "prow", None), P(), P(None, "pcol", "prow", None), P(), P()),
        check_vma=False,
    )
```

profile of v0, /device:TPU:1, one launch (start us, length us, event | category | flops | bytes accessed | tf_op | source)
XLA Modules:
  0.0 760.0 jit_solution(10065821596533365772)
XLA Ops:
  7.2 0.8 convert_element_type.11
  8.1 22.7 %all_gather.9 = f32[4,1,256,128]{3,2,0,1:T(8,128)S(1)} all-gather(f32[4,1,16,128]{3,2,0,1:T(8,128)} %bitcast.74), channel_id=1, replica_groups=mesh['prow'=32,'pcol'=16] {'pcol'}, dimensions={2}, use_global_device_ids=true | all-gather | bytes 557056 | tf_op jit(solution)/shard_map/all_gather | solution.py:49
  31.0 3.1 fusion.4
  34.8 17.4 %all_gather.10 = f32[4,1,256,128]{3,2,0,1:T(8,128)S(1)} all-gather(f32[4,1,16,128]{3,2,0,1:T(8,128)S(1)} %bitcast.75), channel_id=1, replica_groups=mesh['prow'=32,'pcol'=16] {'pcol'}, dimensions={2}, use_global_device_ids=true | all-gather | bytes 557056 | tf_op jit(solution)/shard_map/all_gather | solution.py:50
  52.1 3.1 fusion.7
  55.3 134.7 %all-reduce.9.cloned.1.call-done = f32[8,256,128]{2,1,0:T(8,128)} async-done(((f32[8,256,128]{2,1,0:T(8,128)}), f32[8,256,128]{2,1,0:T(8,128)}) %all-reduce.9.cloned.1.call-update) | async-done | bytes 1048592 | tf_op jit(solution)/shard_map/psum | solution.py:58
  190.0 1.4 negate_multiply_fusion.1
  191.5 1.3 fusion.12
  192.8 2.0 fusion.10
  195.1 1.7 convolution_bitcast_fusion.2
  196.8 157.6 %all-reduce.15.cloned.1.call-done = (f32[256,256]{1,0:T(8,128)}, f32[8,256,128]{2,1,0:T(8,128)}) async-done(((f32[256,256]{1,0:T(8,128)}, f32[8,256,128]{2,1,0:T(8,128)}), (f32[256,256]{1,0:T(8,128)}, f32[8,256,128]{2,1,0:T(8,128)})) %all-reduce.15.cloned.1.call-update) | async-done | bytes 1310736 | tf_op jit(solution)/shard_map/psum | solution.py:66
  354.5 1.4 negate_multiply_fusion
  355.9 1.0 copy-done.3
  356.9 1.3 fusion.11
  358.2 113.8 %all-reduce.11.cloned.1.call-done = f32[256,256]{1,0:T(8,128)} async-done(((f32[256,256]{1,0:T(8,128)}), f32[256,256]{1,0:T(8,128)}) %all-reduce.11.cloned.1.call-update) | async-done | bytes 262160 | tf_op jit(solution)/shard_map/psum | solution.py:67
  472.1 1.0 sub.15
  473.1 1.1 fusion.14
  474.3 157.2 %all-reduce.13.cloned.1.call-done = (f32[256,256]{1,0:T(8,128)}, f32[256,256]{1,0:T(8,128)}) async-done(((f32[256,256]{1,0:T(8,128)}, f32[256,256]{1,0:T(8,128)}), (f32[256,256]{1,0:T(8,128)}, f32[256,256]{1,0:T(8,128)})) %all-reduce.13.cloned.1.call-update) | async-done | bytes 524304 | tf_op jit(solution)/shard_map/psum | solution.py:74
  631.5 35.0 %all_gather.11 = f32[256,256]{1,0:T(8,128)S(1)} all-gather(f32[8,256]{1,0:T(8,128)S(1)} %copy-done.8), channel_id=1, replica_groups=mesh['prow'=32,'pcol'=16] {'prow'}, dimensions={0}, use_global_device_ids=true | all-gather | bytes 270336 | tf_op jit(solution)/shard_map/all_gather | solution.py:51
  666.6 1.4 dynamic-slice_bitcast_fusion.1
  668.0 1.4 dynamic-slice_bitcast_fusion
  669.3 81.0 %all-reduce.17.cloned.1.call-done = (f32[256,256]{1,0:T(8,128)}, f32[256,256]{1,0:T(8,128)}) async-done(((f32[256,256]{1,0:T(8,128)}, f32[256,256]{1,0:T(8,128)}), (f32[256,256]{1,0:T(8,128)}, f32[256,256]{1,0:T(8,128)})) %all-reduce.17.cloned.1.call-update) | async-done | bytes 524304 | tf_op jit(solution)/shard_map/psum | solution.py:75
  750.3 1.0 neg.11
  751.3 2.1 convolution_subtract_fusion
  (40 shorter events, 1.4 us)
Async XLA Ops:
  7.2 23.8 %copy-start = (f32[4,1,128,8,1,128]{5,4,3,2,1,0:T(1,128)S(1)}, f32[4,1,128,8,1,128]{5,4,3,2,1,0:T(1,128)}, u32[]{:S(2)}) copy-start(f32[4,1,128,8,1,128]{5,4,3,2,1,0:T(1,128)} %param.8) | copy-start | bytes 6291460
  7.2 182.8 %all-reduce.9.cloned.1.call-start = ((), (), s32[]{:S(2)}) async-start(), calls=%async_computation | async-start | bytes 2097152 | tf_op jit(solution)/shard_map/psum | solution.py:58
  31.0 3.3 copy-start.10
  31.0 3.8 copy-start.9
  34.1 320.3 %all-reduce.15.cloned.1.call-start = ((), (), s32[]{:S(2)}) async-start(), calls=%async_computation.3 | async-start | bytes 2621440 | tf_op jit(solution)/shard_map/psum | solution.py:66
  55.3 137.5 %copy-start.8 = (f32[8,256]{1,0:T(8,128)S(1)}, f32[8,256]{1,0:T(8,128)}, u32[]{:S(2)}) copy-start(f32[8,256]{1,0:T(8,128)} %param.11) | copy-start | bytes 24580
  190.0 2.8 copy-start.2
  191.4 1.3 copy-start.1
  194.8 277.2 %all-reduce.11.cloned.1.call-start = ((), (), s32[]{:S(2)}) async-start(), calls=%async_computation.1 | async-start | bytes 524288 | tf_op jit(solution)/shard_map/psum | solution.py:67
  196.8 275.3 %copy-start.6 = (f32[256,256]{1,0:T(8,128)S(1)}, f32[256,256]{1,0:T(8,128)}, u32[]{:S(2)}) copy-start(f32[256,256]{1,0:T(8,128)} %param.12) | copy-start | bytes 786436
  354.5 277.0 %all-reduce.13.cloned.1.call-start = ((), (), s32[]{:S(2)}) async-start(), calls=%async_computation.2 | async-start | bytes 1048576 | tf_op jit(solution)/shard_map/psum | solution.py:74
  355.9 1.0 copy-start.3
  358.2 393.1 %copy-start.7 = (f32[256,256]{1,0:T(8,128)S(1)}, f32[256,256]{1,0:T(8,128)}, u32[]{:S(2)}) copy-start(f32[256,256]{1,0:T(8,128)} %param.13) | copy-start | bytes 786436
  473.1 280.4 %copy-start.5 = (f32[256,256]{1,0:T(8,128)}, f32[256,256]{1,0:T(8,128)S(1)}, u32[]{:S(2)}) copy-start(f32[256,256]{1,0:T(8,128)S(1)} %sub.15) | copy-start | bytes 786436
  474.2 276.0 %all-reduce.17.cloned.1.call-start = ((), (), s32[]{:S(2)}) async-start(), calls=%async_computation.4 | async-start | bytes 1048576 | tf_op jit(solution)/shard_map/psum | solution.py:75
  751.3 2.2 copy-start.4
Sparse Core Ops, SparseCore 0:
  34.3 155.6 all-reduce.8
  195.0 159.4 all-reduce.14
  356.9 115.1 all-reduce.10
  475.9 155.5 all-reduce.12
  633.9 116.3 all-reduce.16
where the time goes:
time: 760 us
  waiting for transfers between devices  644 us (85%)
  blocking collectives  75.1 us (10%)
  matrix products  15.9 us (2%)
  between operations  13.9 us (2%)
    psum x1, waiting for transfers between devices, body(): column_a = lax.psum(term_a, 'prow')  158 us
    psum x1, waiting for transfers between devices, body(): cross_col, own_col = lax.psum((cross_term, own_term), 'prow')  157 us
    psum x1, waiting for transfers between devices, body(): row_a = -lax.psum(part_a, 'prow') * cmask_a  135 us
    psum x1, waiting for transfers between devices, body(): own_a = dinv_first - lax.psum(column_a, 'pcol')  114 us
    psum x1, waiting for transfers between devices, body(): cross_sum, own_sum = lax.psum((cross_col, own_col), 'pcol')  81 us
    all_gather x1, blocking collectives, body(): coupling_full = lax.all_gather(coupling, 'prow', axis=0, tiled=True)  35 us
    all_gather x1, blocking collectives, body(): panel_a = lax.all_gather(panel_first, 'pcol', axis=2, tiled=True)[:, 0]  22.7 us
    all_gather x1, blocking collectives, body(): panel_b = lax.all_gather(panel_second, 'pcol', axis=2, tiled=True)[:, 0]  17.4 us
  transfers between devices with their start and end apart: 5, of which 5 were waited for; matrix products, arithmetic and copies ran while one was open for 1% of the time, Pallas kernels for 0%

commit v1 on v0

--- a/solution.py
+++ b/solution.py
@@ -1,7 +1,16 @@
+import functools
 import jax
 import jax.numpy as jnp
 from jax import lax
 from jax.sharding import PartitionSpec as P
+
+
+def track_the_chunk(x_in, link_axis):
+    r1 = lax.all_gather(x_in, link_axis).sum(axis=0)
+    return r1
+
+
+sector_set = functools.partial(track_the_chunk, link_axis="prow")
 
 
 def body(
@@ -63,7 +72,7 @@
     mine_a = my_rows(row_a)
     mine_b = my_rows(row_b)
     term_a = jnp.einsum("rwy,rvy->wv", chosen_a, panel_a, precision=highest) * diagonal
-    column_a = lax.psum(term_a, "prow")
+    column_a = sector_set(term_a)
     own_a = dinv_first - lax.psum(column_a, "pcol")
     own_rows = lax.dynamic_slice_in_dim(own_a, prow_index * slab, slab, 0)
     cross_term = (

time: 760 us -> 867 us (1.14)
  waiting for transfers between devices: 644 us -> 742 us
    all_gather x0 -> x1, waiting for transfers between devices: none -> 107 us  [track_the_chunk(): r1 = lax.all_gather(x_in, link_axis).sum(axis=0)]
  transfers between devices with their start and end apart: 5 -> 6, of which waited for: 5 -> 6; matrix products, arithmetic and copies ran while one was open for 1% -> 2% of each run, Pallas kernels for 0% -> 0%
where the time goes in v1:
time: 867 us; the launch traced here: 866 us
  waiting for transfers between devices  742 us (86%)
  blocking collectives  75.3 us (9%)
  matrix products  17.9 us (2%)
  between operations  14.2 us (2%)
  other arithmetic  11.1 us (1%)
    psum x1, waiting for transfers between devices, body(): cross_col, own_col = lax.psum((cross_term, own_term), 'prow')  158 us
    psum x1, waiting for transfers between devices, body(): row_b = -lax.psum(part_b + carried, 'prow') * cmask_b  154 us
    psum x1, waiting for transfers between devices, body(): row_a = -lax.psum(part_a, 'prow') * cmask_a  135 us
    psum x1, waiting for transfers between devices, body(): own_a = dinv_first - lax.psum(column_a, 'pcol')  108 us
    all_gather x1, waiting for transfers between devices, track_the_chunk(): r1 = lax.all_gather(x_in, link_axis).sum(axis=0)  107 us
    psum x1, waiting for transfers between devices, body(): cross_sum, own_sum = lax.psum((cross_col, own_col), 'pcol')  80.7 us
    all_gather x1, blocking collectives, body(): coupling_full = lax.all_gather(coupling, 'prow', axis=0, tiled=True)  35.1 us
    all_gather x1, blocking collectives, body(): panel_a = lax.all_gather(panel_first, 'pcol', axis=2, tiled=True)[:, 0]  22.8 us
  transfers between devices with their start and end apart: 6, of which 6 were waited for; matrix products, arithmetic and copies ran while one was open for 2% of the time, Pallas kernels for 0%

profile of v1, /device:TPU:1, one launch (start us, length us, event | category | flops | bytes accessed | tf_op | source)
XLA Modules:
  0.0 866.1 jit_solution(9964754084088746575)
XLA Ops:
  7.2 22.8 %all_gather.15 = f32[4,1,256,128]{3,2,0,1:T(8,128)S(1)} all-gather(f32[4,1,16,128]{3,2,0,1:T(8,128)} %bitcast.76), channel_id=1, replica_groups=mesh['prow'=32,'pcol'=16] {'pcol'}, dimensions={2}, use_global_device_ids=true | all-gather | bytes 557056 | tf_op jit(solution)/shard_map/all_gather | solution.py:58
  31.0 3.1 fusion.4
  34.8 17.4 %all_gather.18 = f32[4,1,256,128]{3,2,0,1:T(8,128)S(1)} all-gather(f32[4,1,16,128]{3,2,0,1:T(8,128)S(1)} %bitcast.77), channel_id=1, replica_groups=mesh['prow'=32,'pcol'=16] {'pcol'}, dimensions={2}, use_global_device_ids=true | all-gather | bytes 557056 | tf_op jit(solution)/shard_map/all_gather | solution.py:59
  52.1 3.1 fusion.7
  55.2 134.8 %all-reduce.8.cloned.1.call-done = f32[8,256,128]{2,1,0:T(8,128)} async-done(((f32[8,256,128]{2,1,0:T(8,128)}), f32[8,256,128]{2,1,0:T(8,128)}) %all-reduce.8.cloned.1.call-update) | async-done | bytes 1048592 | tf_op jit(solution)/shard_map/psum | solution.py:67
  190.0 1.4 negate_multiply_fusion.1
  191.5 1.0 copy-done.1
  192.5 2.0 fusion.10
  194.6 2.4 fusion.12
  197.3 1.7 convolution_bitcast_fusion.2
  199.0 153.8 %all-reduce.12.cloned.1.call-done = f32[8,256,128]{2,1,0:T(8,128)} async-done(((f32[8,256,128]{2,1,0:T(8,128)}), f32[8,256,128]{2,1,0:T(8,128)}) %all-reduce.12.cloned.1.call-update) | async-done | bytes 1048592 | tf_op jit(solution)/shard_map/psum | solution.py:69
  352.8 2.3 negate_multiply_fusion
  355.1 107.2 %all-gather.3.cloned.1.call-done = f32[8192,256]{1,0:T(8,128)} async-done(((f32[256,256]{1,0:T(8,128)}), f32[8192,256]{1,0:T(8,128)}) %all-gather.3.cloned.1.call-update) | async-done | bytes 8388624 | tf_op jit(solution)/shard_map/all_gather | solution.py:9
  462.4 4.7 reduce_sum.9
  467.1 2.4 fusion.11
  469.5 108.3 %all-reduce.10.cloned.1.call-done = f32[256,256]{1,0:T(8,128)} async-done(((f32[256,256]{1,0:T(8,128)}), f32[256,256]{1,0:T(8,128)}) %all-reduce.10.cloned.1.call-update) | async-done | bytes 262160 | tf_op jit(solution)/shard_map/psum | solution.py:76
  577.8 1.0 sub.15
  578.8 1.1 fusion.14
  580.0 157.6 %all-reduce.14.cloned.1.call-done = (f32[256,256]{1,0:T(8,128)}, f32[256,256]{1,0:T(8,128)}) async-done(((f32[256,256]{1,0:T(8,128)}, f32[256,256]{1,0:T(8,128)}), (f32[256,256]{1,0:T(8,128)}, f32[256,256]{1,0:T(8,128)})) %all-reduce.14.cloned.1.call-update) | async-done | bytes 524304 | tf_op jit(solution)/shard_map/psum | solution.py:83
  737.6 35.1 %all_gather.19 = f32[256,256]{1,0:T(8,128)S(1)} all-gather(f32[8,256]{1,0:T(8,128)S(1)} %copy-done.7), channel_id=1, replica_groups=mesh['prow'=32,'pcol'=16] {'prow'}, dimensions={0}, use_global_device_ids=true | all-gather | bytes 270336 | tf_op jit(solution)/shard_map/all_gather | solution.py:60
  772.8 1.4 dynamic-slice_bitcast_fusion.1
  774.1 1.4 dynamic-slice_bitcast_fusion
  775.5 80.7 %all-reduce.16.cloned.1.call-done = (f32[256,256]{1,0:T(8,128)}, f32[256,256]{1,0:T(8,128)}) async-done(((f32[256,256]{1,0:T(8,128)}, f32[256,256]{1,0:T(8,128)}), (f32[256,256]{1,0:T(8,128)}, f32[256,256]{1,0:T(8,128)})) %all-reduce.16.cloned.1.call-update) | async-done | bytes 524304 | tf_op jit(solution)/shard_map/psum | solution.py:84
  857.2 2.1 convolution_subtract_fusion
  (42 shorter events, 3.1 us)
Async XLA Ops:
  7.2 23.8 %copy-start = (f32[4,1,128,8,1,128]{5,4,3,2,1,0:T(1,128)S(1)}, f32[4,1,128,8,1,128]{5,4,3,2,1,0:T(1,128)}, u32[]{:S(2)}) copy-start(f32[4,1,128,8,1,128]{5,4,3,2,1,0:T(1,128)} %param.8) | copy-start | bytes 6291460
  7.2 182.8 %all-reduce.8.cloned.1.call-start = ((), (), s32[]{:S(2)}) async-start(), calls=%async_computation | async-start | bytes 2097152 | tf_op jit(solution)/shard_map/psum | solution.py:67
  31.0 3.3 copy-start.9
  31.0 3.8 copy-start.8
  34.2 318.6 %all-reduce.12.cloned.1.call-start = ((), (), s32[]{:S(2)}) async-start(), calls=%async_computation.2 | async-start | bytes 2097152 | tf_op jit(solution)/shard_map/psum | solution.py:69
  52.1 140.4 %copy-start.7 = (f32[8,256]{1,0:T(8,128)S(1)}, f32[8,256]{1,0:T(8,128)}, u32[]{:S(2)}) copy-start(f32[8,256]{1,0:T(8,128)} %param.11) | copy-start | bytes 24580
  190.0 2.5 copy-start.2
  191.5 1.1 copy-start.1
  194.6 267.8 %all-gather.3.cloned.1.call-start = ((), (), s32[]{:S(2)}) async-start(), calls=%async_computation.3 | async-start | bytes 8650752 | tf_op jit(solution)/shard_map/all_gather | solution.py:9
  197.0 380.7 %all-reduce.10.cloned.1.call-start = ((), (), s32[]{:S(2)}) async-start(), calls=%async_computation.1 | async-start | bytes 524288 | tf_op jit(solution)/shard_map/psum | solution.py:76
  462.4 115.4 %copy-start.5 = (f32[256,256]{1,0:T(8,128)S(1)}, f32[256,256]{1,0:T(8,128)}, u32[]{:S(2)}) copy-start(f32[256,256]{1,0:T(8,128)} %param.12) | copy-start | bytes 786436
  467.1 270.6 %all-reduce.14.cloned.1.call-start = ((), (), s32[]{:S(2)}) async-start(), calls=%async_computation.4 | async-start | bytes 1048576 | tf_op jit(solution)/shard_map/psum | solution.py:83
  469.5 387.7 %copy-start.6 = (f32[256,256]{1,0:T(8,128)S(1)}, f32[256,256]{1,0:T(8,128)}, u32[]{:S(2)}) copy-start(f32[256,256]{1,0:T(8,128)} %param.13) | copy-start | bytes 786436
  578.8 280.5 %copy-start.4 = (f32[256,256]{1,0:T(8,128)}, f32[256,256]{1,0:T(8,128)S(1)}, u32[]{:S(2)}) copy-start(f32[256,256]{1,0:T(8,128)S(1)} %sub.15) | copy-start | bytes 786436
  579.9 276.2 %all-reduce.16.cloned.1.call-start = ((), (), s32[]{:S(2)}) async-start(), calls=%async_computation.5 | async-start | bytes 1048576 | tf_op jit(solution)/shard_map/psum | solution.py:84
  857.1 2.2 copy-start.3
Sparse Core Ops, SparseCore 0:
  34.3 155.6 all-reduce.7
  194.7 158.0 all-reduce.11
  356.6 105.7 all-gather.2
  467.2 110.5 all-reduce.9
  582.0 155.5 all-reduce.13
  739.9 116.2 all-reduce.15
